TPU v7x, 128 devices: a whole 4x4x4 slice. The times are simulated.
128 devices in a mesh: grp: 8 (over z, core), blk: 16 (over y, x).
Axes of the slice: x: 4, y: 4, z: 4, core: 2. Of those that a mesh axis runs over, the one named last changes fastest.
Arguments:
- matrix: float32 [32768, 4096], P(('grp', 'blk')), as said below
- signs: int32 [32768], P(('grp', 'blk')), may hold values from -1 to 1, as said below
- tile_rows: int32 [8, 16, 128], P('grp'), may hold values from -1 to 255, as said below
- tile_owner: int32 [8, 16], P('grp'), may hold values from 0 to 15, as said below
Outputs:
- r_top: float32 [768, 4096], P(None, 'blk')
- trailing: float32 [32768, 4096], P(('grp', 'blk'))
Inputs may be any that keep to these rules, and one draw needn't show every extreme that they name: `tile_rows`: slot s of every tile samples a row of the device at blk index s mod 16 of the same grp index; each grp index has padding and reaches the largest row index. `tile_owner`: within each grp index no owner holds more than 2 tiles, and some owner holds exactly 2. `signs`: each entry is -1 or 1. `matrix`: entries of order one with per-column scales.
All inputs are finite; a program needn't handle non-finite values.
Results may differ from a plain program's by a relative error of at most 0.0001.
Values sent between devices are 32-bit elements; how exact they have to be, the bound alone decides.
No kernel may reach another device: no remote copies, remote signals or barrier semaphores. Data moves between devices by JAX's collectives and lax.ppermute only.
A program may use at most 128 MiB of HBM per device.

v0:
```python
import math

import jax
import jax.numpy as jnp
from jax import lax
from jax.sharding import PartitionSpec as P

TILE = 128
MAXT = 2
PANEL = 128
NPAN = 6


def swapped(block, axis, stride):
    count = lax.axis_size(axis)
    route = []
    for low in range(count):
        high = low | 1 << stride
        if high != low and high < count:
            route += [(low, high), (high, low)]
    return lax.ppermute(block, axis, route)


def hadamard(order):
    index = jnp.arange(order, dtype=jnp.int32)
    total = jnp.zeros((order, order), jnp.int32)
    for level in range(order.bit_length() - 1):
        upper = index // 2**level % 2
        total = total + upper[:, None] * upper[None, :]
    return (1 - 2 * (total % 2)).astype(jnp.float32)


def lower_solve(lower, right):
    return lax.linalg.triangular_solve(lower, right, left_side=True, lower=True)


def body(matrix, signs, tile_rows, tile_owner):
    rows_dev, width = matrix.shape
    groups = lax.axis_size("grp")
    owners = lax.axis_size("blk")
    signed = matrix * signs.astype(jnp.float32)[:, None]
    local = jnp.dot(
        hadamard(rows_dev),
        signed,
        precision=lax.Precision.HIGHEST,
        preferred_element_type=jnp.float32,
    )
    position = lax.axis_index("grp")
    mixed = local
    for level in range(groups.bit_length() - 1):
        partner = swapped(mixed, "grp", level)
        upper = position // 2**level % 2 == 1
        mixed = jnp.where(upper, partner - mixed, mixed + partner)
    mixed = mixed * (1.0 / math.sqrt(groups * rows_dev))
    owner_list = tile_owner[0]
    row_lists = tile_rows[0]
    tiles = owner_list.shape[0]
    per_source = TILE // owners
    me_blk = lax.axis_index("blk")
    picked = row_lists.reshape(tiles, per_source, owners)
    selector = jnp.arange(owners, dtype=jnp.int32) == me_blk
    wanted = jnp.sum(jnp.where(selector[None, None, :], picked, 0), axis=2)
    taken = jnp.take(mixed, jnp.maximum(wanted, 0).reshape(-1), axis=0).reshape(
        tiles, per_source, width
    )
    taken = jnp.where((wanted >= 0)[..., None], taken, 0.0)
    same = owner_list[:, None] == owner_list[None, :]
    order = jnp.arange(tiles, dtype=jnp.int32)
    rank = jnp.sum((same & (order[None, :] < order[:, None])).astype(jnp.int32), axis=1)
    target = owner_list * MAXT + rank
    outgoing = jnp.zeros((owners * MAXT, per_source, width), jnp.float32).at[target].set(taken)
    outgoing = outgoing.reshape(owners, MAXT, per_source, 1, width)
    arrived = lax.all_to_all(outgoing, "blk", split_axis=0, concat_axis=3, tiled=True)
    current = arrived.reshape(MAXT * TILE, width)
    columns = jnp.arange(width, dtype=jnp.int32)
    factor_rows = []
    for panel_index in range(NPAN):
        start = panel_index * PANEL
        panel = current[:, start : start + PANEL]
        partial_products = jnp.dot(
            panel.T, current, precision=lax.Precision.HIGHEST, preferred_element_type=jnp.float32
        )
        products = lax.psum(partial_products, ("grp", "blk"))
        lower = jnp.linalg.cholesky(products[:, start : start + PANEL])
        row_block = lower_solve(lower, products)
        row_block = jnp.where(columns[None, :] >= start, row_block, 0.0)
        basis = lower_solve(lower, panel.T).T
        current = current - jnp.dot(
            basis, row_block, precision=lax.Precision.HIGHEST, preferred_element_type=jnp.float32
        )
        factor_rows.append(row_block)
    upper_rows = jnp.concatenate(factor_rows, axis=0)
    stacked = upper_rows * (1.0 / math.sqrt(groups * owners * TILE))
    share = width // owners
    r_top = lax.dynamic_slice_in_dim(stacked, me_blk * share, share, 1)
    return (r_top, current)


def solution(mesh):
    in_specs = (P(("grp", "blk"), None), P(("grp", "blk")), P("grp", None, None), P("grp", None))
    out_specs = (P(None, "blk"), P(("grp", "blk"), None))
    return jax.shard_map(body, mesh=mesh, in_specs=in_specs, out_specs=out_specs, check_vma=False)
```

profile of v0, /device:TPU:1, one launch (start us, length us, event | category | flops | bytes accessed | tf_op | source)
XLA Modules:
  0.0 1479.8 jit_solution(7333357297100313493)
XLA Ops:
  7.9 8.2 fusion
  16.1 1.4 collective-permute-start
  17.6 7.1 collective-permute-done
  24.7 6.4 add_select_fusion.1
  31.1 1.7 collective-permute-start.1
  32.8 90.9 %collective-permute-done.1 = f32[256,4096]{1,0:T(8,128)} collective-permute-done((f32[256,4096]{1,0:T(8,128)}, f32[256,4096]{1,0:T(8,128)}, u32[]{:S(2)}, u32[]{:S(2)}) %collective-permute-start.1) | collective-permute-done | bytes 4194336 | tf_op jit(solution)/shard_map/ppermute | solution.py:21
  123.7 6.4 add_select_fusion
  130.2 3.1 collective-permute-start.2
  134.1 89.2 %collective-permute-done.2 = f32[256,4096]{1,0:T(8,128)} collective-permute-done((f32[256,4096]{1,0:T(8,128)}, f32[256,4096]{1,0:T(8,128)}, u32[]{:S(2)}, u32[]{:S(2)}) %collective-permute-start.2) | collective-permute-done | bytes 4194336 | tf_op jit(solution)/shard_map/ppermute | solution.py:21
  223.3 6.5 select_multiply_fusion
  229.8 5.6 gather_fusion
  235.5 1.9 fusion.2
  237.4 2.5 broadcast_in_dim.106
  239.9 3.7 scatter_fusion
  243.6 57.6 %all_to_all.15 = f32[16,2,8,1,4096]{4,2,1,3,0:T(8,128)S(1)} all-to-all(f32[16,2,8,1,4096]{4,2,1,3,0:T(8,128)} %bitcast.155), channel_id=1, replica_groups=mesh['grp'=8,'blk'=16] {'blk'}, dimensions={0} | all-to-all | bytes 8388608 | tf_op jit(solution)/shard_map/all_to_all | solution.py:73
  301.1 2.4 copy.46
  303.6 2.0 copy-done
  305.6 8.0 fusion.59
  314.2 149.6 %all-reduce.7.cloned.1.call-done = f32[128,4096]{0,1:T(8,128)} async-done(((f32[128,4096]{0,1:T(8,128)}), f32[128,4096]{0,1:T(8,128)}) %all-reduce.7.cloned.1.call-update) | async-done | bytes 2097168 | tf_op jit(solution)/shard_map/psum | solution.py:83
  465.6 11.7 cholesky.104
  478.7 9.8 custom-call.18
  488.5 1.4 fusion.22
  489.9 4.9 constant_dynamic-update-slice_fusion.5
  494.7 3.6 convolution_subtract_fusion.5
  498.4 2.0 copy-done.4
  500.4 8.6 fusion.56
  509.1 148.8 %all-reduce.9.cloned.1.call-done = f32[128,4096]{0,1:T(8,128)} async-done(((f32[128,4096]{0,1:T(8,128)}), f32[128,4096]{0,1:T(8,128)}) %all-reduce.9.cloned.1.call-update) | async-done | bytes 2097168 | tf_op jit(solution)/shard_map/psum | solution.py:83
  659.6 11.7 cholesky.115
  672.7 9.8 custom-call.20
  682.5 1.4 fusion.20
  683.9 4.8 constant_dynamic-update-slice_fusion.4
  688.7 3.6 convolution_subtract_fusion.4
  692.4 2.0 copy-done.6
  694.4 8.7 fusion.53
  703.7 148.3 %all-reduce.11.cloned.1.call-done = f32[128,4096]{0,1:T(8,128)} async-done(((f32[128,4096]{0,1:T(8,128)}), f32[128,4096]{0,1:T(8,128)}) %all-reduce.11.cloned.1.call-update) | async-done | bytes 2097168 | tf_op jit(solution)/shard_map/psum | solution.py:83
  853.8 11.7 cholesky.126
  866.8 9.8 custom-call.22
  876.7 1.4 fusion.18
  878.0 4.9 constant_dynamic-update-slice_fusion.3
  882.9 3.6 convolution_subtract_fusion.3
  886.6 2.0 copy-done.8
  888.6 8.6 fusion.50
  897.9 148.1 %all-reduce.13.cloned.1.call-done = f32[128,4096]{0,1:T(8,128)} async-done(((f32[128,4096]{0,1:T(8,128)}), f32[128,4096]{0,1:T(8,128)}) %all-reduce.13.cloned.1.call-update) | async-done | bytes 2097168 | tf_op jit(solution)/shard_map/psum | solution.py:83
  1047.8 11.7 cholesky.137
  1060.9 9.8 custom-call.24
  1072.1 4.9 constant_dynamic-update-slice_fusion.2
  1077.0 3.6 convolution_subtract_fusion.2
  1080.6 2.0 copy-done.10
  1082.6 8.5 fusion.47
  1091.3 148.8 %all-reduce.15.cloned.1.call-done = f32[128,4096]{0,1:T(8,128)} async-done(((f32[128,4096]{0,1:T(8,128)}), f32[128,4096]{0,1:T(8,128)}) %all-reduce.15.cloned.1.call-update) | async-done | bytes 2097168 | tf_op jit(solution)/shard_map/psum | solution.py:83
  1241.8 11.7 cholesky.148
  1254.9 9.8 custom-call.26
  1264.7 1.4 fusion.14
  1266.1 4.9 constant_dynamic-update-slice_fusion.1
  1271.0 3.6 convolution_subtract_fusion.1
  1274.7 2.0 copy-done.2
  1276.7 8.6 fusion.44
  1285.3 148.8 %all-reduce.17.cloned.1.call-done = f32[128,4096]{0,1:T(8,128)} async-done(((f32[128,4096]{0,1:T(8,128)}), f32[128,4096]{0,1:T(8,128)}) %all-reduce.17.cloned.1.call-update) | async-done | bytes 2097168 | tf_op jit(solution)/shard_map/psum | solution.py:83
  1436.0 11.7 cholesky.159
  1449.0 10.0 custom-call.28
  1459.1 1.4 fusion.12
  1460.4 4.8 constant_dynamic-update-slice_fusion
  1465.3 2.1 dynamic-slice_multiply_fusion
  1467.3 5.2 convolution_subtract_fusion
  (90 shorter events, 23.6 us)
Async XLA Ops:
  7.2 456.7 %all-reduce.7.cloned.1.call-start = ((), (), s32[]{:S(2)}) async-start(), calls=%async_computation.1 | async-start | bytes 4194304 | tf_op jit(solution)/shard_map/psum | solution.py:83
  16.1 8.6 collective-permute-start
  31.1 92.6 %collective-permute-start.1 = (f32[256,4096]{1,0:T(8,128)}, f32[256,4096]{1,0:T(8,128)}, u32[]{:S(2)}, u32[]{:S(2)}) collective-permute-start(f32[256,4096]{1,0:T(8,128)} %add_select_fusion.1), channel_id=1, source_target_pairs={{0,32},{32,0},{16,48},{48,16},{64,96},{96,64},{80,112},{112,80},{1... | collective-permute-start | bytes 12582920 | tf_op jit(solution)/shard_map/ppermute | solution.py:21
  32.8 100.5 %copy-start.12 = (s32[1,16,128]{2,1,0:T(8,128)S(1)}, s32[1,16,128]{2,1,0:T(8,128)}, u32[]{:S(2)}) copy-start(s32[1,16,128]{2,1,0:T(8,128)} %param.11) | copy-start | bytes 24580
  32.8 101.0 %copy-start.13 = (s32[1,16]{1,0:T(1,128)S(1)}, s32[1,16]{1,0:T(1,128)}, u32[]{:S(2)}) copy-start(s32[1,16]{1,0:T(1,128)} %param.12) | copy-start | bytes 196
  130.2 93.1 %collective-permute-start.2 = (f32[256,4096]{1,0:T(8,128)}, f32[256,4096]{1,0:T(8,128)}, u32[]{:S(2)}, u32[]{:S(2)}) collective-permute-start(f32[256,4096]{1,0:T(8,128)} %add_select_fusion), channel_id=1, source_target_pairs={{0,64},{64,0},{16,80},{80,16},{32,96},{96,32},{48,112},{112,48},{1... | collective-permute-start | bytes 12582920 | tf_op jit(solution)/shard_map/ppermute | solution.py:21
  303.6 2.0 copy-start
  313.7 344.2 %all-reduce.9.cloned.1.call-start = ((), (), s32[]{:S(2)}) async-start(), calls=%async_computation.2 | async-start | bytes 4194304 | tf_op jit(solution)/shard_map/psum | solution.py:83
  488.5 6.3 copy-start.1
  498.4 2.0 copy-start.4
  509.0 343.0 %all-reduce.11.cloned.1.call-start = ((), (), s32[]{:S(2)}) async-start(), calls=%async_computation.3 | async-start | bytes 4194304 | tf_op jit(solution)/shard_map/psum | solution.py:83
  682.5 6.2 copy-start.5
  692.4 2.0 copy-start.6
  703.2 342.9 %all-reduce.13.cloned.1.call-start = ((), (), s32[]{:S(2)}) async-start(), calls=%async_computation.4 | async-start | bytes 4194304 | tf_op jit(solution)/shard_map/psum | solution.py:83
  876.6 6.3 copy-start.7
  886.6 2.0 copy-start.8
  897.2 342.9 %all-reduce.15.cloned.1.call-start = ((), (), s32[]{:S(2)}) async-start(), calls=%async_computation.5 | async-start | bytes 4194304 | tf_op jit(solution)/shard_map/psum | solution.py:83
  1070.7 6.3 copy-start.9
  1080.6 2.0 copy-start.10
  1091.2 343.0 %all-reduce.17.cloned.1.call-start = ((), (), s32[]{:S(2)}) async-start(), calls=%async_computation.6 | async-start | bytes 4194304 | tf_op jit(solution)/shard_map/psum | solution.py:83
  1264.7 6.3 copy-start.11
  1274.7 2.0 copy-start.2
  1459.1 8.3 copy-start.3
Sparse Core Ops, SparseCore 0:
  313.8 149.9 all-reduce.6
  509.1 148.6 all-reduce.8
  703.3 148.6 all-reduce.10
  897.3 148.6 all-reduce.12
  1091.3 148.6 all-reduce.14
  1285.4 148.6 all-reduce.16
where the time goes:
time: 1490 us; the launch traced here: 1480 us
  waiting for transfers between devices  1080 us (72%)
  other arithmetic  167 us (11%)
  matrix products  120 us (8%)
  blocking collectives  57.6 us (4%)
  local copies, waits for them, and re-layouts  32.1 us (2%)
  between operations  15 us (1%)
    psum x6, waiting for transfers between devices, body(): products = lax.psum(partial_products, ('grp', 'blk'))  892 us
    ppermute x3, waiting for transfers between devices, swapped(): return lax.ppermute(block, axis, route)  187 us
    another operation x18, other arithmetic, body(): lower = jnp.linalg.cholesky(products[:, start:start + PANEL])  74.3 us
    another operation x12, other arithmetic, lower_solve(): return lax.linalg.triangular_solve(lower, right, left_side=True, lower=True)  63 us
    all_to_all x1, blocking collectives, body(): lax.all_to_all(outgoing, 'blk', split_axis=0, concat_axis=3, tiled=True)  57.6 us
    dot_general x6, matrix products, body(): jnp.dot(panel.T, current, precision=lax.Precision.HIGHEST, preferred_elem...  51.1 us
    another operation x12, matrix products, lower_solve(): return lax.linalg.triangular_solve(lower, right, left_side=True, lower=True)  37.4 us
  transfers between devices with their start and end apart: 9, of which 9 were waited for; matrix products, arithmetic and copies ran while one was open for 0% of the time, Pallas kernels for 0%

commit v1 on v0

v1 whole, which is shorter than its diff:
```python
import functools
import math

import jax
import jax.numpy as jnp
from jax import lax
from jax.experimental import pallas as pl
from jax.experimental.pallas import tpu as pltpu
from jax.sharding import PartitionSpec as P

TILE = 128
MAXT = 2
PANEL = 128
NPAN = 6
WIDE = PANEL * NPAN
HI = lax.Precision.HIGHEST


def dot(a, b, dims, precision=HI):
    return lax.dot_general(
        a, b, (dims, ((), ())), precision=precision, preferred_element_type=jnp.float32
    )


def inverse_factor(block):
    n = block.shape[0]
    sub = lax.broadcasted_iota(jnp.int32, (n, n), 0)
    lane = lax.broadcasted_iota(jnp.int32, (n, n), 1)
    sub8 = lax.broadcasted_iota(jnp.int32, (8, n), 0)
    left, right = block, (sub == lane).astype(jnp.float32)
    rows = []
    for step in range(n // 8):
        base = 8 * step
        top_left, top_right = left[:8], right[:8]
        cols = [jnp.broadcast_to(top_left[:, base + k : base + k + 1], (8, n)) for k in range(8)]
        pivots = jnp.zeros((8, n), jnp.float32)
        for j in range(8):
            pivot = jnp.broadcast_to(cols[j][j : j + 1], (8, n))
            pivots = jnp.where(sub8 == j, pivot, pivots)
            if j == 7:
                break
            factor = jnp.where(sub8 > j, cols[j] * (1.0 / pivot), 0.0)
            for k in range(j + 1, 8):
                cols[k] = cols[k] - factor * cols[k][j : j + 1]
            top_left = top_left - factor * top_left[j : j + 1]
            top_right = top_right - factor * top_right[j : j + 1]
        scale = lax.rsqrt(pivots)
        top_left, top_right = top_left * scale, top_right * scale
        rows.append(top_right)
        if step < n // 8 - 1:
            turned = top_left.T
            left, right = left[8:], right[8:]
            for k in range(8):
                col = turned[base + 8 :, k : k + 1]
                left = left - col * top_left[k : k + 1]
                right = right - col * top_right[k : k + 1]
    return jnp.concatenate(rows, axis=0)


def factor_kernel(gram_ref, inv_ref, work_ref):
    n = gram_ref.shape[0]
    work_ref[...] = gram_ref[...]
    inv_ref[...] = jnp.zeros_like(inv_ref)
    for low in range(0, n, PANEL):
        high = low + PANEL
        inverse = inverse_factor(work_ref[low:high, low:high])
        inv_ref[low:high, low:high] = inverse
        if low:
            inv_ref[low:high, :low] = dot(inverse, inv_ref[low:high, :low], ((1,), (0,)))
        if high < n:
            upper = dot(inverse, work_ref[low:high, high:], ((1,), (0,)))
            work_ref[high:, high:] -= dot(upper, upper, ((0,), (0,)))
            inv_ref[high:, :high] -= dot(upper, inv_ref[low:high, :high], ((0,), (0,)))


def inverse_of_factor(gram):
    n = gram.shape[0]
    return pl.pallas_call(
        factor_kernel,
        out_shape=jax.ShapeDtypeStruct((n, n), jnp.float32),
        in_specs=[pl.BlockSpec(memory_space=pltpu.VMEM)],
        out_specs=pl.BlockSpec(memory_space=pltpu.VMEM),
        scratch_shapes=[pltpu.VMEM((n, n), jnp.float32)],
        compiler_params=pltpu.CompilerParams(vmem_limit_bytes=32 * 2**20),
        cost_estimate=pl.CostEstimate(flops=10**9, bytes_accessed=6 * 2**20, transcendentals=0),
    )(gram)


def grp_swap(x, d):
    return lax.ppermute(x, "grp", [(i, i ^ d) for i in range(lax.axis_size("grp"))])


def parity(x):
    return lax.population_count(x) % 2


def body(matrix, signs, tile_rows, tile_owner):
    rows_dev, width = matrix.shape
    groups = lax.axis_size("grp")
    owners = lax.axis_size("blk")
    me = lax.axis_index("grp")
    me_blk = lax.axis_index("blk")
    zed, core = me // 2, me % 2
    tiles = tile_owner.shape[1]
    per_source = TILE // owners
    lanes = 128
    slots = width // (groups * lanes)
    part = slots * lanes
    picked = tiles * per_source

    wanted = tile_rows[0].reshape(tiles, per_source, owners)
    selector = jnp.arange(owners, dtype=jnp.int32) == me_blk
    wanted = jnp.sum(jnp.where(selector, wanted, 0), axis=2).reshape(1, picked)
    wanted = lax.all_gather(wanted, "grp", tiled=True)

    signed = matrix * signs.astype(jnp.float32)[:, None]
    pieces = signed.reshape(rows_dev, slots, groups // 2, 2, lanes).transpose(2, 3, 0, 1, 4)
    pieces = pieces.reshape(groups // 2, 2, rows_dev, part)
    got = []
    for d in range(groups // 2):
        mine = lax.dynamic_index_in_dim(pieces, zed ^ d, 0, keepdims=False)
        got.append(grp_swap(mine, 2 * d) if d else mine)
    got = jnp.stack(got)
    keep = lax.dynamic_index_in_dim(got, core, 1, keepdims=False)
    give = lax.dynamic_index_in_dim(got, 1 - core, 1, keepdims=False)
    mixed = jnp.stack([keep, grp_swap(give, 1)], axis=1).reshape(groups, rows_dev, part)
    for level in range(groups.bit_length() - 1):
        mixed = mixed.reshape(groups >> (level + 1), 2, 1 << level, rows_dev, part)
        low, high = mixed[:, 0], mixed[:, 1]
        mixed = jnp.stack([low + high, low - high], axis=1)
    mixed = mixed.reshape(groups, rows_dev, part)

    index = jnp.arange(rows_dev, dtype=jnp.int32)
    odd = parity(jnp.maximum(wanted, 0)[:, :, None] & index)
    odd = odd + parity(jnp.arange(groups, dtype=jnp.int32) & me)[:, None, None]
    select = (1 - 2 * (odd % 2)).astype(jnp.float32)
    select = jnp.where((wanted >= 0)[:, :, None], select, 0.0)
    sampled = jnp.einsum(
        "gsi,gic->gsc", select, mixed, precision=HI, preferred_element_type=jnp.float32
    ) * (1.0 / math.sqrt(groups * rows_dev))

    mine = sampled[:, :, :lanes]
    got = jnp.stack([grp_swap(mine, 2 * d) if d else mine for d in range(groups // 2)])
    got = jnp.stack([got, grp_swap(got, 1)], axis=1).reshape(groups, groups * picked, lanes)
    lead = jnp.concatenate(
        [lax.dynamic_index_in_dim(got, me ^ t, 0, keepdims=False) for t in range(NPAN)], axis=1
    )

    rest = sampled.reshape(groups * picked, part)
    partial = dot(lead, rest, ((0,), (0,)))
    share = WIDE // owners
    partial = partial.reshape(owners, share, part)
    gram = jnp.sum(lax.all_to_all(partial, "blk", 0, 0, tiled=True), axis=0)
    corner = lax.all_gather(gram[:, :lanes], ("grp", "blk"), tiled=True)
    corner = corner.reshape(groups, WIDE, lanes)
    gram = lax.all_gather(gram, ("grp", "blk"), tiled=True).reshape(groups, WIDE, part)

    back = sampled.reshape(groups // 2, 2, picked, part)
    got = []
    for d in range(groups // 2):
        mine = lax.dynamic_index_in_dim(back, zed ^ d, 0, keepdims=False)
        got.append(grp_swap(mine, 2 * d) if d else mine)
    got = jnp.stack(got)
    keep = lax.dynamic_index_in_dim(got, core, 1, keepdims=False)
    give = lax.dynamic_index_in_dim(got, 1 - core, 1, keepdims=False)
    got = jnp.stack([keep, grp_swap(give, 1)], axis=1).reshape(groups, picked, slots, lanes)
    home = jnp.stack(
        [lax.dynamic_index_in_dim(got, me ^ t, 0, keepdims=False) for t in range(groups)], axis=2
    ).reshape(tiles, per_source, width)
    owner_list = tile_owner[0]
    same = owner_list[:, None] == owner_list[None, :]
    order = jnp.arange(tiles, dtype=jnp.int32)
    rank = jnp.sum((same & (order[None, :] < order[:, None])).astype(jnp.int32), axis=1)
    target = owner_list * MAXT + rank
    outgoing = jnp.zeros((owners * MAXT, per_source, width), jnp.float32).at[target].set(home)
    outgoing = outgoing.reshape(owners, MAXT, per_source, 1, width)
    arrived = lax.all_to_all(outgoing, "blk", split_axis=0, concat_axis=3, tiled=True)
    current = arrived.reshape(MAXT * TILE, width)

    corner = jnp.concatenate([corner[t] for t in range(NPAN)], axis=1)
    inverse = inverse_of_factor(corner)
    basis = dot(current[:, :WIDE], inverse, ((1,), (1,)))
    weights = dot(basis, inverse, ((1,), (0,)))
    taken = jnp.einsum(
        "rk,ckn->rcn", weights, gram, precision=HI, preferred_element_type=jnp.float32
    )
    taken = taken.reshape(MAXT * TILE, groups, slots, lanes).transpose(0, 2, 1, 3)
    trailing = current - taken.reshape(MAXT * TILE, width)

    wide = width // owners
    per = wide // lanes
    first = me_blk * per
    own = lax.dynamic_slice(
        gram, (first % groups, 0, first // groups * lanes), (per, WIDE, lanes)
    )
    own = own.transpose(1, 0, 2).reshape(WIDE, wide)
    r_top = dot(inverse, own, ((1,), (0,)))
    column = me_blk * wide + jnp.arange(wide, dtype=jnp.int32)
    start = jnp.arange(WIDE, dtype=jnp.int32) // PANEL * PANEL
    r_top = jnp.where(column[None, :] >= start[:, None], r_top, 0.0)
    r_top = r_top * (1.0 / math.sqrt(groups * owners * TILE))
    return (r_top, trailing)


def solution(mesh):
    in_specs = (P(("grp", "blk"), None), P(("grp", "blk")), P("grp", None, None), P("grp", None))
    out_specs = (P(None, "blk"), P(("grp", "blk"), None))
    return jax.shard_map(body, mesh=mesh, in_specs=in_specs, out_specs=out_specs, check_vma=False)
```

time: 1490 us -> 428 us (0.29)
  waiting for transfers between devices: 1080 us -> 163 us
  other arithmetic: 167 us -> 27.6 us
  matrix products: 120 us -> 33.7 us
  local copies, waits for them, and re-layouts: 32.1 us -> 79.6 us
  Pallas kernels: 0 us -> 40.9 us
  blocking collectives: 57.6 us -> 39.2 us
    psum x6 -> x0, waiting for transfers between devices: 892 us -> none  [body(): products = lax.psum(partial_products, ('grp', 'blk'))]
    another operation x30 -> x8, other arithmetic: 137 us -> 12.6 us  [the longest x2 3.78 us: body(): jnp.stack([got, grp_swap(got, 1)], axis=1)]
    ppermute x3 -> x12, waiting for transfers between devices: 187 us -> 97.4 us  [grp_swap(): lax.ppermute(x, 'grp', [(i, i ^ d) for i in range(lax.axis_size('grp'))])]
    all_to_all x0 -> x1, waiting for transfers between devices: none -> 64.9 us  [body(): lax.all_to_all(outgoing, 'blk', split_axis=0, concat_axis=3, tiled=True)]
    dot_general x13 -> x6, matrix products: 82.7 us -> 33.7 us  [the longest x4 15 us: dot(): lax.dot_general(a, b, (dims, ((), ())), precision=precision, preferred_el...]
    pallas_call x0 -> x1, Pallas kernels: none -> 40.9 us  [inverse_of_factor(): pl.pallas_call(factor_kernel, out_shape=jax.ShapeDtypeStruct((n, n), jnp....]
    another operation x12 -> x0, matrix products: 37.4 us -> none  [lower_solve(): return lax.linalg.triangular_solve(lower, right, left_side=True, lower=True)]
    all_to_all x1, blocking collectives: 57.6 us -> 28.7 us  [body(): gram = jnp.sum(lax.all_to_all(partial, 'blk', 0, 0, tiled=True), axis=0)]
  transfers between devices with their start and end apart: 9 -> 15, of which waited for: 9 -> 9; matrix products, arithmetic and copies ran while one was open for 0% -> 9% of each run, Pallas kernels for 0% -> 10%
where the time goes in v1:
time: 428 us; the launch traced here: 420 us
  waiting for transfers between devices  163 us (38%)
  local copies, waits for them, and re-layouts  79.6 us (19%)
  Pallas kernels  40.9 us (10%)
  blocking collectives  39.2 us (9%)
  matrix products  33.7 us (8%)
  other arithmetic  27.6 us (6%)
  starting transfers between devices  20.9 us (5%)
  between operations  14.9 us (3%)
    ppermute x12, waiting for transfers between devices, grp_swap(): lax.ppermute(x, 'grp', [(i, i ^ d) for i in range(lax.axis_size('grp'))])  97.4 us
    all_to_all x1, waiting for transfers between devices, body(): lax.all_to_all(outgoing, 'blk', split_axis=0, concat_axis=3, tiled=True)  64.9 us
    pallas_call x1, Pallas kernels, inverse_of_factor(): pl.pallas_call(factor_kernel, out_shape=jax.ShapeDtypeStruct((n, n), jnp....  40.9 us
    all_to_all x1, blocking collectives, body(): gram = jnp.sum(lax.all_to_all(partial, 'blk', 0, 0, tiled=True), axis=0)  28.7 us
    ppermute x12, starting transfers between devices, grp_swap(): lax.ppermute(x, 'grp', [(i, i ^ d) for i in range(lax.axis_size('grp'))])  15.9 us
    unnamed x27, local copies, waits for them, and re-layouts  15.1 us
    dot_general x4, matrix products, dot(): lax.dot_general(a, b, (dims, ((), ())), precision=precision, preferred_el...  15 us
    dot_general x1, matrix products, body(): jnp.einsum('rk,ckn->rcn', weights, gram, precision=HI, preferred_element_...  14.6 us
  transfers between devices with their start and end apart: 15, of which 9 were waited for; matrix products, arithmetic and copies ran while one was open for 9% of the time, Pallas kernels for 10%

profile of v1, /device:TPU:1, one launch (start us, length us, event | category | flops | bytes accessed | tf_op | source)
XLA Modules:
  0.0 419.8 jit_solution(10952105938011748914)
XLA Ops:
  7.2 0.7 convert_element_type.10
  7.9 5.6 %copy.38 = f32[256,4096]{0,1:T(8,128)} copy(f32[256,4096]{1,0:T(8,128)} %param.4) | data formatting | bytes 8388608 | tf_op args[0]
  13.5 2.5 broadcast_multiply_fusion
  16.0 2.4 copy.39
  18.3 3.6 constant_dynamic-slice_fusion.11
  22.0 4.6 %collective-permute-start.2 = (f32[2,256,512]{1,2,0:T(8,128)}, f32[2,256,512]{1,2,0:T(8,128)}, u32[]{:S(2)}, u32[]{:S(2)}) collective-permute-start(f32[2,256,512]{1,2,0:T(8,128)} %get-tuple-element.13), channel_id=1, source_target_pairs={{0,96},{16,112},{32,64},{48,80},{64,32},{80,48},{96,0},{112,16},{1... | collective-permute-start | bytes 3145736 | tf_op jit(solution)/shard_map/ppermute | solution.py:90
  27.1 45.1 %collective-permute-done.2 = f32[2,256,512]{1,2,0:T(8,128)} collective-permute-done((f32[2,256,512]{1,2,0:T(8,128)}, f32[2,256,512]{1,2,0:T(8,128)}, u32[]{:S(2)}, u32[]{:S(2)}) %collective-permute-start.2) | collective-permute-done | bytes 1048608 | tf_op jit(solution)/shard_map/ppermute | solution.py:90
  72.4 2.3 pad_maximum_fusion
  74.7 1.7 constant_dynamic-slice_fusion.10
  76.4 1.5 collective-permute-start.3
  78.4 10.5 %all-gather = s32[8,1,128]{2,1,0:T(1,128)S(1)} all-gather(s32[1,1,128]{2,1,0:T(1,128)S(1)} %reshape.191), channel_id=1, replica_groups=mesh['grp'=8,'blk'=16] {'grp'}, dimensions={0}, use_global_device_ids=true | all-gather | bytes 4608 | tf_op jit(solution)/shard_map/all_gather | solution.py:114
  89.0 2.0 maximum_bitcast_fusion
  91.7 2.3 pad_maximum_fusion.1
  94.0 5.2 %copy.40 = f32[2,2,2,256,512]{4,3,2,1,0:T(8,128)} copy(f32[2,2,2,256,512]{3,4,1,0,2:T(8,128)} %pad_maximum_fusion.1) | data formatting | bytes 8388608 | tf_op jit(solution)/shard_map/stack | solution.py:130
  99.2 2.8 slice_add_fusion
  102.5 4.0 convolution_multiply_fusion
  106.6 0.7 collective-permute-start.5
  107.3 2.7 collective-permute-start.6
  110.0 11.6 %collective-permute-done.5 = f32[8,128,128]{2,1,0:T(8,128)S(1)} collective-permute-done((f32[8,128,128]{2,1,0:T(8,128)S(1)}, f32[8,128,128]{2,1,0:T(8,128)S(1)}, u32[]{:S(2)}, u32[]{:S(2)}) %collective-permute-start.5) | collective-permute-done | bytes 524320 | tf_op jit(solution)/shard_map/ppermute | solution.py:90
  121.6 8.2 %collective-permute-done.4 = f32[8,128,128]{2,1,0:T(8,128)S(1)} collective-permute-done((f32[8,128,128]{2,1,0:T(8,128)S(1)}, f32[8,128,128]{2,1,0:T(8,128)S(1)}, u32[]{:S(2)}, u32[]{:S(2)}) %collective-permute-start.4) | collective-permute-done | bytes 524320 | tf_op jit(solution)/shard_map/ppermute | solution.py:90
  129.7 3.6 collective-permute-done.6
  133.3 1.8 fusion.38
  135.1 0.7 collective-permute-start.7
  135.8 4.1 collective-permute-done.7
  139.9 2.0 pad_maximum_fusion.3
  142.7 1.7 copy-done.2
  144.4 2.4 copy.42
  146.8 6.7 %fusion.39 = f32[16,48,512]{2,1,0:T(8,128)S(1)} fusion(f32[16,48,1024]{2,1,0:T(8,128)S(1)} %bitcast.137, f32[1024,512,1]{1,0,2:T(8,128)} %bitcast.138), kind=kOutput, calls=%fused_computation.116 | convolution fusion | flops 4831838208 | bytes 6815744 | tf_op jit(solution)/shard_map/dot_general | solution.py:20
  153.4 28.7 %all_to_all.20 = f32[16,48,512]{2,1,0:T(8,128)} all-to-all(f32[16,48,512]{2,1,0:T(8,128)S(1)} %fusion.39), channel_id=1, replica_groups=mesh['grp'=8,'blk'=16] {'blk'}, dimensions={0} | all-to-all | bytes 3145728 | tf_op jit(solution)/shard_map/all_to_all | solution.py:153
  182.2 1.5 reduce_sum.30
  183.7 0.6 slice.73
  184.4 0.7 all-gather.6.cloned.1.call-update
  185.8 0.6 collective-permute-start.9
  186.4 2.3 collective-permute-start.8
  188.7 22.6 %collective-permute-done.10 = f32[2,128,512]{2,1,0:T(8,128)S(1)} collective-permute-done((f32[2,128,512]{2,1,0:T(8,128)S(1)}, f32[2,128,512]{2,1,0:T(8,128)S(1)}, u32[]{:S(2)}, u32[]{:S(2)}) %collective-permute-start.10) | collective-permute-done | bytes 524320 | tf_op jit(solution)/shard_map/ppermute | solution.py:90
  211.7 1.9 collective-permute-start.11
  213.8 2.1 collective-permute-done.11
  215.9 1.6 pad_maximum_fusion.7
  217.5 1.9 reshape.178
  219.4 1.0 constant_dynamic-slice_fusion.12
  220.4 6.2 %stack.143 = f32[128,4,8,128]{3,2,1,0:T(8,128)} concatenate(f32[128,4,1,128]{3,2,1,0:T(1,128)} %bitcast.152, f32[128,4,1,128]{3,2,1,0:T(1,128)} %bitcast.151, f32[128,4,1,128]{3,2,1,0:T(1,128)} %bitcast.150, f32[128,4,1,128]{3,2,1,0:T(1,128)S(1)} %bitcast.149, f32[128,4,1,128]{3,2,1,0:T(1,128)S(1)} %bitcast.148, f32[128,4,1,128]{3,2,1,0:T(1,128)S(1)} %bitcast.147, ...), dimensions={2} | concatenate | bytes 4194304 | tf_op jit(solution)/shard_map/stack | solution.py:167
  226.6 1.7 reshape.187
  228.4 2.5 broadcast_in_dim.42
  230.9 3.7 scatter_fusion
  234.5 5.0 %all-to-all-start.1 = ((f32[16,2,8,1,4096]{4,2,1,3,0:T(8,128)}), f32[16,2,8,1,4096]{4,2,1,3,0:T(8,128)}, u32[]{:S(2)}, u32[]{:S(2)}) async-start(f32[16,2,8,1,4096]{4,2,1,3,0:T(8,128)} %bitcast.123), calls=%async_computation.1 | async-start | bytes 8388608 | tf_op jit(solution)/shard_map/all_to_all | solution.py:177
  239.5 64.9 %all-to-all-done.1 = f32[16,2,8,1,4096]{4,2,1,3,0:T(8,128)} async-done(((f32[16,2,8,1,4096]{4,2,1,3,0:T(8,128)}), f32[16,2,8,1,4096]{4,2,1,3,0:T(8,128)}, u32[]{:S(2)}, u32[]{:S(2)}) %all-to-all-start.1) | async-done | bytes 4194336 | tf_op jit(solution)/shard_map/all_to_all | solution.py:177
  304.4 6.6 %copy.45 = f32[16,2,8,1,4096]{4,0,2,1,3:T(8,128)} copy(f32[16,2,8,1,4096]{4,2,1,3,0:T(8,128)} %all-to-all-done.1) | data formatting | bytes 8388608 | tf_op jit(solution)/shard_map/all_to_all | solution.py:177
  311.0 1.0 slice_dynamic-update-slice_fusion.5
  312.0 1.0 slice_dynamic-update-slice_fusion.4
  313.1 1.0 slice_dynamic-update-slice_fusion.3
  314.1 1.0 slice_dynamic-update-slice_fusion.2
  315.1 1.0 slice_dynamic-update-slice_fusion.1
  316.2 1.0 slice_dynamic-update-slice_fusion.gram_ref
  317.2 40.9 %shard_map.59 = f32[768,768]{1,0:T(8,128)S(1)} custom-call(f32[768,768]{1,0:T(8,128)S(1)} %slice_dynamic-update-slice_fusion.gram_ref), custom_call_target="tpu_custom_call" | custom-call | flops 1000000000 | bytes 6291456 | tf_op jit(solution)/shard_map/pallas_call | solution.py:78
  358.1 3.3 fusion.16
  361.4 2.2 convolution_bitcast_fusion.1
  363.6 2.1 constant_dynamic-slice_fusion.9
  365.7 2.4 copy.50
  368.0 12.7 %copy.46 = f32[8,512,768]{2,1,0:T(8,128)} copy(f32[8,512,768]{1,2,0:T(8,128)} %bitcast.130) | data formatting | bytes 25165824 | tf_op jit(solution)/shard_map/rk,ckn->rcn/dot_general | solution.py:184
  380.7 14.6 %convolution_bitcast_fusion = f32[256,4,8,128]{0,3,1,2:T(8,128)S(1)} fusion(f32[256,768,1,1]{1,0,3,2:T(8,128)S(1)} %convolution_bitcast_fusion.1, f32[8,4,128,768]{3,2,1,0:T(8,128)} %bitcast.122), kind=kOutput, calls=%fused_computation.8 | convolution fusion | flops 9663676416 | bytes 17563648 | tf_op jit(solution)/shard_map/rk,ckn->rcn/dot_general | solution.py:184
  395.3 2.5 copy.47
  397.8 5.6 %copy.48 = f32[256,4096]{1,0:T(8,128)} copy(f32[256,4096]{0,1:T(8,128)} %bitcast.128) | data formatting | bytes 8388608 | tf_op jit(solution)/shard_map/reshape | solution.py:188
  403.4 6.2 %bitcast_subtract_fusion = f32[256,4096]{1,0:T(8,128)} fusion(f32[256,4096]{1,0:T(8,128)} %copy.48, f32[16,2,8,1,4096]{4,0,2,1,3:T(8,128)} %copy.45), kind=kLoop, calls=%fused_computation.110 | loop fusion | flops 1048576 | bytes 12582912 | tf_op jit(solution)/shard_map/sub | solution.py:188
  409.6 2.9 fusion.1
  (52 shorter events, 4.6 us)
Async XLA Ops:
  7.2 303.9 %all-gather.4.cloned.1.call-start = ((), (), s32[]{:S(2)}) async-start(), calls=%async_computation.2 | async-start | bytes 3170304 | tf_op jit(solution)/shard_map/all_gather | solution.py:154
  22.0 50.3 %collective-permute-start.2 = (f32[2,256,512]{1,2,0:T(8,128)}, f32[2,256,512]{1,2,0:T(8,128)}, u32[]{:S(2)}, u32[]{:S(2)}) collective-permute-start(f32[2,256,512]{1,2,0:T(8,128)} %get-tuple-element.13), channel_id=1, source_target_pairs={{0,96},{16,112},{32,64},{48,80},{64,32},{80,48},{96,0},{112,16},{1... | collective-permute-start | bytes 3145736 | tf_op jit(solution)/shard_map/ppermute | solution.py:90
  26.5 45.7 %collective-permute-start.1 = (f32[2,256,512]{1,2,0:T(8,128)S(1)}, f32[2,256,512]{1,2,0:T(8,128)}, u32[]{:S(2)}, u32[]{:S(2)}) collective-permute-start(f32[2,256,512]{1,2,0:T(8,128)S(1)} %get-tuple-element.14), channel_id=1, source_target_pairs={{0,64},{16,80},{32,96},{48,112},{64,0},{80,16},{96,32},{112,48},{1... | collective-permute-start | bytes 3145736 | tf_op jit(solution)/shard_map/ppermute | solution.py:90
  26.5 45.8 %collective-permute-start = (f32[2,256,512]{1,2,0:T(8,128)S(1)}, f32[2,256,512]{1,2,0:T(8,128)}, u32[]{:S(2)}, u32[]{:S(2)}) collective-permute-start(f32[2,256,512]{1,2,0:T(8,128)S(1)} %get-tuple-element.15), channel_id=1, source_target_pairs={{0,32},{16,48},{32,0},{48,16},{64,96},{80,112},{96,64},{112,80},{1... | collective-permute-start | bytes 3145736 | tf_op jit(solution)/shard_map/ppermute | solution.py:90
  74.7 3.2 copy-start.5
  76.4 12.6 %collective-permute-start.3 = (f32[4,256,512]{1,2,0:T(8,128)}, f32[4,256,512]{1,2,0:T(8,128)}, u32[]{:S(2)}, u32[]{:S(2)}) collective-permute-start(f32[4,256,512]{1,2,0:T(8,128)} %get-tuple-element.11), channel_id=1, source_target_pairs={{0,16},{16,0},{32,48},{48,32},{64,80},{80,64},{96,112},{112,96},{1... | collective-permute-start | bytes 6291464 | tf_op jit(solution)/shard_map/ppermute | solution.py:90
  106.5 28.6 %copy-start = (f32[8,128,512]{2,1,0:T(8,128)}, f32[8,128,512]{2,1,0:T(8,128)S(1)}, u32[]{:S(2)}) copy-start(f32[8,128,512]{2,1,0:T(8,128)S(1)} %convolution_multiply_fusion) | copy-start | bytes 6291460
  106.6 14.9 %collective-permute-start.5 = (f32[8,128,128]{2,1,0:T(8,128)S(1)}, f32[8,128,128]{2,1,0:T(8,128)S(1)}, u32[]{:S(2)}, u32[]{:S(2)}) collective-permute-start(f32[8,128,128]{2,1,0:T(8,128)S(1)} %get-tuple-element.33), channel_id=1, source_target_pairs={{0,64},{16,80},{32,96},{48,112},{64,0},{80,16},{96,32},{112,48},{1... | collective-permute-start | bytes 1572872 | tf_op jit(solution)/shard_map/ppermute | solution.py:90
  107.3 22.4 %collective-permute-start.4 = (f32[8,128,128]{2,1,0:T(8,128)S(1)}, f32[8,128,128]{2,1,0:T(8,128)S(1)}, u32[]{:S(2)}, u32[]{:S(2)}) collective-permute-start(f32[8,128,128]{2,1,0:T(8,128)S(1)} %get-tuple-element.33), channel_id=1, source_target_pairs={{0,32},{16,48},{32,0},{48,16},{64,96},{80,112},{96,64},{112,80},{1... | collective-permute-start | bytes 1572872 | tf_op jit(solution)/shard_map/ppermute | solution.py:90
  107.3 26.0 %collective-permute-start.6 = (f32[8,128,128]{2,1,0:T(8,128)S(1)}, f32[8,128,128]{2,1,0:T(8,128)S(1)}, u32[]{:S(2)}, u32[]{:S(2)}) collective-permute-start(f32[8,128,128]{2,1,0:T(8,128)S(1)} %get-tuple-element.33), channel_id=1, source_target_pairs={{0,96},{16,112},{32,64},{48,80},{64,32},{80,48},{96,0},{112,16},{1... | collective-permute-start | bytes 1572872 | tf_op jit(solution)/shard_map/ppermute | solution.py:90
  135.1 4.8 %collective-permute-start.7 = (f32[4,8,128,128]{3,2,1,0:T(8,128)}, f32[4,8,128,128]{3,2,1,0:T(8,128)}, u32[]{:S(2)}, u32[]{:S(2)}) collective-permute-start(f32[4,8,128,128]{3,2,1,0:T(8,128)} %get-tuple-element.31), channel_id=1, source_target_pairs={{0,16},{16,0},{32,48},{48,32},{64,80},{80,64},{96,112},{112,96},{1... | collective-permute-start | bytes 6291464 | tf_op jit(solution)/shard_map/ppermute | solution.py:90
  142.7 1.7 copy-start.2
  153.4 31.7 %copy-start.1 = (f32[8,128,512]{2,1,0:T(8,128)S(1)}, f32[8,128,512]{2,1,0:T(8,128)}, u32[]{:S(2)}) copy-start(f32[8,128,512]{2,1,0:T(8,128)} %copy-done) | copy-start | bytes 6291460
  183.7 0.7 copy-start.4
  184.4 179.2 %all-gather.6.cloned.1.call-start = ((), (), s32[]{:S(2)}) async-start(), calls=%async_computation.3 | async-start | bytes 12681216 | tf_op jit(solution)/shard_map/all_gather | solution.py:156
  185.4 25.9 %collective-permute-start.10 = (f32[2,128,512]{2,1,0:T(8,128)S(1)}, f32[2,128,512]{2,1,0:T(8,128)S(1)}, u32[]{:S(2)}, u32[]{:S(2)}) collective-permute-start(f32[2,128,512]{2,1,0:T(8,128)S(1)} %get-tuple-element.27), channel_id=1, source_target_pairs={{0,96},{16,112},{32,64},{48,80},{64,32},{80,48},{96,0},{112,16},{1... | collective-permute-start | bytes 1572872 | tf_op jit(solution)/shard_map/ppermute | solution.py:90
  185.8 25.5 %collective-permute-start.9 = (f32[2,128,512]{2,1,0:T(8,128)S(1)}, f32[2,128,512]{2,1,0:T(8,128)S(1)}, u32[]{:S(2)}, u32[]{:S(2)}) collective-permute-start(f32[2,128,512]{2,1,0:T(8,128)S(1)} %get-tuple-element.28), channel_id=1, source_target_pairs={{0,64},{16,80},{32,96},{48,112},{64,0},{80,16},{96,32},{112,48},{1... | collective-permute-start | bytes 1572872 | tf_op jit(solution)/shard_map/ppermute | solution.py:90
  186.4 24.9 %collective-permute-start.8 = (f32[2,128,512]{2,1,0:T(8,128)S(1)}, f32[2,128,512]{2,1,0:T(8,128)S(1)}, u32[]{:S(2)}, u32[]{:S(2)}) collective-permute-start(f32[2,128,512]{2,1,0:T(8,128)S(1)} %get-tuple-element.29), channel_id=1, source_target_pairs={{0,32},{16,48},{32,0},{48,16},{64,96},{80,112},{96,64},{112,80},{1... | collective-permute-start | bytes 1572872 | tf_op jit(solution)/shard_map/ppermute | solution.py:90
  211.5 2.1 copy-start.6
  211.7 4.2 collective-permute-start.11
  234.5 69.9 %all-to-all-start.1 = ((f32[16,2,8,1,4096]{4,2,1,3,0:T(8,128)}), f32[16,2,8,1,4096]{4,2,1,3,0:T(8,128)}, u32[]{:S(2)}, u32[]{:S(2)}) async-start(f32[16,2,8,1,4096]{4,2,1,3,0:T(8,128)} %bitcast.123), calls=%async_computation.1 | async-start | bytes 8388608 | tf_op jit(solution)/shard_map/all_to_all | solution.py:177
  403.4 6.2 %copy-start.3 = (f32[2,768,128]{1,2,0:T(8,128)S(1)}, f32[2,768,128]{1,2,0:T(8,128)}, u32[]{:S(2)}) copy-start(f32[2,768,128]{1,2,0:T(8,128)} %copy.50) | copy-start | bytes 2359300
Sparse Core Ops, SparseCore 0:
  184.5 79.8 all-gather.3
  267.4 91.4 all-gather.5
